TPU v7x, 32 devices: a whole 2x2x4 slice. The times are simulated.
32 devices in a mesh: docs: 2 (over y), seq: 4 (over z), head: 4 (over x, core).
Axes of the slice: x: 2, y: 2, z: 4, core: 2. Of those that a mesh axis runs over, the one named last changes fastest.
Arguments:
- tokens: bfloat16 [6144, 1024], P(('docs', 'seq'), 'head'), parts along dimension 0, may hold values from -6 to 6
- norm_gain: float32 [1024], replicated, may hold values from 0.1 to 1.9
- w_query: bfloat16 [1024, 1024], P(None, 'head'), may hold values from -5.0375 to 5.0375
- w_key: bfloat16 [1024, 1024], P(None, 'head'), may hold values from -5.0375 to 5.0375
- w_value: bfloat16 [1024, 1024], P(None, 'head'), may hold values from -0.1875 to 0.1875
- w_out: bfloat16 [1024, 1024], P('head'), may hold values from -0.25 to 0.25
- cluster_ids: int32 [16, 6144, 1], P('head', ('docs', 'seq')), parts along dimension 1, may hold values from 0 to 255; in each aligned block of 768 rows (0 to 767, 768 to 1535, ..., all dimensions but the last counted through in order) at most 6 rows name the same one
Outputs:
- layer_out: bfloat16 [6144, 1024], P(('docs', 'seq'), 'head'), parts along dimension 0
There are 2 independent parts, one for each index of `docs`. A program takes and returns all parts, laid end to end along the dimension named above; an argument that names none is the same for every part. Nothing has to cross between parts.
Inputs may be any that keep to these rules, and one draw needn't show every extreme that they name: `cluster_ids`: among the 768 tokens of one index of seq, at most 6 name the same cluster in one head, a bound that some block reaches so.
All inputs are finite; a program needn't handle non-finite values.
Results may differ from a plain program's by a relative error of at most 0.0055.
Values may be sent and summed in bfloat16 or wider, within the bound.
A program may use at most 64 MiB of HBM per device.

v0:
```python
import jax
import jax.numpy as jnp
from jax import lax
from jax.sharding import PartitionSpec as P

HEAD_DIM = 64
CLUSTERS = 256
CAPACITY = 6


def attend_block(received, marks, n_seq):
    count = received.shape[1]
    span = n_seq * CAPACITY
    parts = received.reshape(3, count, span, HEAD_DIM)
    live = marks.reshape(count, span) > 0.5
    scores = jnp.einsum(
        "csd,ctd->cst", parts[0], parts[1], preferred_element_type=jnp.float32
    ) * HEAD_DIM ** (-0.5)
    scores = jnp.where(live[:, None, :], scores, jnp.float32(-1e30))
    top = jnp.max(scores, axis=-1, keepdims=True)
    expo = jnp.exp(scores - top)
    weights = (expo / jnp.sum(expo, axis=-1, keepdims=True)).astype(jnp.bfloat16)
    result = jnp.einsum(
        "cst,ctd->csd", weights, parts[2], preferred_element_type=jnp.float32
    ).astype(jnp.bfloat16)
    return result.reshape(count, n_seq, CAPACITY * HEAD_DIM)


def place_head(operands):
    head_slot, head_parts = operands
    columns = jnp.arange(CLUSTERS * CAPACITY, dtype=jnp.int32)
    onehot = (head_slot[:, None] == columns[None, :]).astype(jnp.bfloat16)
    placed = jnp.einsum(
        "ts,ctd->csd", onehot, head_parts, preferred_element_type=jnp.float32
    ).astype(jnp.bfloat16)
    filled = jnp.sum(onehot, axis=0, dtype=jnp.float32).astype(jnp.bfloat16)
    return (placed, filled)


def fetch_head(operands):
    head_slot, head_back = operands
    columns = jnp.arange(CLUSTERS * CAPACITY, dtype=jnp.int32)
    onehot = (head_slot[:, None] == columns[None, :]).astype(jnp.bfloat16)
    return jnp.dot(onehot, head_back, preferred_element_type=jnp.float32).astype(jnp.bfloat16)


def on_device(tokens, norm_gain, w_query, w_key, w_value, w_out, cluster_ids):
    n_seq = lax.axis_size("seq")
    tok = tokens.shape[0]
    heads_here = w_query.shape[1] // HEAD_DIM
    owned = CLUSTERS // n_seq
    rows = lax.all_gather(tokens, "head", axis=1, tiled=True)
    inputs = rows.astype(jnp.float32)
    square = jnp.mean(inputs * inputs, axis=-1, keepdims=True)
    normed = (inputs * lax.rsqrt(square + 1e-05) * norm_gain).astype(jnp.bfloat16)
    queries = jnp.dot(normed, w_query, preferred_element_type=jnp.float32).astype(jnp.bfloat16)
    keys = jnp.dot(normed, w_key, preferred_element_type=jnp.float32).astype(jnp.bfloat16)
    values = jnp.dot(normed, w_value, preferred_element_type=jnp.float32).astype(jnp.bfloat16)
    ids = cluster_ids[:, :, 0]
    owner = ids // owned
    within = ids % owned
    positions = jnp.arange(tok, dtype=jnp.int32)
    earlier = positions[None, :] < positions[:, None]
    same = (ids[:, :, None] == ids[:, None, :]) & earlier[None, :, :]
    rank = jnp.sum(same.astype(jnp.int32), axis=2)
    slot_local = (within * n_seq + owner) * CAPACITY + rank
    stacked = jnp.stack([queries, keys, values]).reshape(3, tok, heads_here, HEAD_DIM)
    stacked = stacked.transpose(2, 0, 1, 3)
    placed, filled = lax.map(place_head, (slot_local, stacked))
    outgoing = placed.transpose(1, 0, 2, 3).reshape(
        3, heads_here * owned, n_seq, CAPACITY * HEAD_DIM
    )
    out_marks = filled.reshape(1, heads_here * owned, n_seq, CAPACITY)
    received, in_marks = (
        lax.all_to_all(outgoing, "seq", split_axis=2, concat_axis=2, tiled=True),
        lax.all_to_all(out_marks, "seq", split_axis=2, concat_axis=2, tiled=True),
    )
    result = attend_block(received, in_marks, n_seq)
    returned = lax.all_to_all(result, "seq", split_axis=1, concat_axis=1, tiled=True)
    back_heads = returned.reshape(heads_here, CLUSTERS * CAPACITY, HEAD_DIM)
    fetched = lax.map(fetch_head, (slot_local, back_heads))
    attended = fetched.transpose(1, 0, 2).reshape(tok, heads_here * HEAD_DIM)
    partial_sums = jnp.dot(attended, w_out, preferred_element_type=jnp.float32)
    share = lax.psum_scatter(partial_sums, "head", scatter_dimension=1, tiled=True)
    return (tokens.astype(jnp.float32) + share).astype(jnp.bfloat16)


def solution(mesh):
    return jax.shard_map(
        on_device,
        mesh=mesh,
        in_specs=(
            P(("docs", "seq"), "head"),
            P(),
            P(None, "head"),
            P(None, "head"),
            P(None, "head"),
            P("head", None),
            P("head", ("docs", "seq"), None),
        ),
        out_specs=P(("docs", "seq"), "head"),
        check_vma=False,
    )
```

profile of v0, /device:TPU:0, one launch (start us, length us, event | category | flops | bytes accessed | tf_op | source)
XLA Modules:
  0.0 229.2 jit_solution(15783100895475844290)
XLA Ops:
  8.2 2.2 convert_reduce_fusion
  11.1 20.3 %all-gather.2.cloned.1.call-done = bf16[768,1024]{1,0:T(8,128)(2,1)} async-done(((bf16[768,256]{1,0:T(8,128)(2,1)}), bf16[768,1024]{1,0:T(8,128)(2,1)}) %all-gather.2.cloned.1.call-update) | async-done | bytes 1572880 | tf_op jit(solution)/shard_map/all_gather | solution.py:52
  33.4 2.3 %convolution_convert_fusion.1 = bf16[768,256]{0,1:T(8,128)(2,1)S(1)} fusion(bf16[1024,256]{1,0:T(8,128)(2,1)} %param.15, bf16[768,1024]{1,0:T(8,128)(2,1)} %all-gather.2.cloned.1.call-done, f32[1024]{0:T(1024)S(1)} %copy-done.8, f32[768]{0:T(1024)S(1)} %add_rsqrt_fusion), kind=kOutput, calls=%fused_computation.40 | convolution fusion | flops 405995520 | bytes 2497536 | tf_op jit(solution)/shard_map/dot_general | solution.py:58
  38.8 11.4 %while.24 = (s32[]{:T(128)}, bf16[4,3,1536,64]{2,3,1,0:T(8,128)(2,1)S(1)}, bf16[4,1536]{1,0:T(4,128)(2,1)S(1)}, bf16[4,3,768,64]{2,3,1,0:T(8,128)(2,1)}, s32[4,768]{1,0:T(4,128)S(1)}, /*index=5*/s32[]{:T(128)}, s32[]{:T(128)}) while((s32[]{:T(128)}, bf16[4,3,1536,64]{2,3,1,0:T(8,128)(2,1)S(1)}, bf16[4,1536]{1,0:T(4,128)(2,1)S(1)}, ...), condition=%wide.region_4.5_spmd, body=%wide.region_2.4_spmd.sunk | while | flops 457996800 | bytes 914517 | solution.py:69
  38.8 2.2 fusion.69
  41.6 2.2 fusion.69
  44.5 2.2 fusion.69
  47.4 2.2 fusion.69
  51.5 4.6 %all-to-all-start = ((bf16[1,256,4,6]{1,3,0,2:T(8,128)(2,1)}), bf16[1,256,4,6]{1,3,0,2:T(8,128)(2,1)S(1)}, u32[]{:S(2)}, u32[]{:S(2)}) async-start(bf16[1,256,4,6]{1,3,0,2:T(8,128)(2,1)} %copy.46), calls=%async_computation | async-start | bytes 32768 | tf_op jit(solution)/shard_map/all_to_all | solution.py:76
  56.1 3.9 %copy.48 = bf16[3,4,1536,64]{3,2,1,0:T(8,128)(2,1)} copy(bf16[3,4,1536,64]{2,3,0,1:T(8,128)(2,1)S(1)} %bitcast.76) | data formatting | bytes 4718592 | tf_op jit(solution)/shard_map/transpose | solution.py:70
  60.0 6.7 %reshape.66 = bf16[3,256,4,384]{3,2,1,0:T(4,128)(2,1)S(1)} reshape(bf16[3,4,1536,64]{3,2,1,0:T(8,128)(2,1)} %copy.48) | data formatting | bytes 4718592 | tf_op jit(solution)/shard_map/reshape | solution.py:70
  68.6 5.1 %all-to-all-start.1 = ((bf16[3,256,4,384]{3,1,0,2:T(8,128)(2,1)}), bf16[3,256,4,384]{3,1,0,2:T(8,128)(2,1)S(1)}, u32[]{:S(2)}, u32[]{:S(2)}) async-start(bf16[3,256,4,384]{3,1,0,2:T(8,128)(2,1)} %copy.49), calls=%async_computation.1 | async-start | bytes 4718592 | tf_op jit(solution)/shard_map/all_to_all | solution.py:75
  73.8 53.5 %all-to-all-done.1 = bf16[3,256,4,384]{3,1,0,2:T(8,128)(2,1)S(1)} async-done(((bf16[3,256,4,384]{3,1,0,2:T(8,128)(2,1)}), bf16[3,256,4,384]{3,1,0,2:T(8,128)(2,1)S(1)}, u32[]{:S(2)}, u32[]{:S(2)}) %all-to-all-start.1) | async-done | bytes 2359328 | tf_op jit(solution)/shard_map/all_to_all | solution.py:75
  136.3 4.9 %fusion.47 = (f32[256,24]{1,0:T(8,128)S(1)}, f32[256,24,24]{1,2,0:T(8,128)}) fusion(pred[256,24]{1,0:T(8,128)(4,1)S(1)} %copy.47, bf16[256,24,64]{2,1,0:T(8,128)(2,1)} %copy.52, bf16[256,24,64]{2,1,0:T(8,128)(2,1)} %copy.53), kind=kOutput, calls=%fused_computation.63 | convolution fusion | flops 19464216 | bytes 2193408 | tf_op jit(solution)/shard_map/sub | solution.py:21
  141.2 4.1 %convolution_convert_fusion = bf16[256,24,64]{2,1,0:T(8,128)(2,1)} fusion(bf16[256,24,64]{2,1,0:T(8,128)(2,1)S(1)} %copy-done.4, f32[256,24,24]{1,2,0:T(8,128)} %get-tuple-element.118, f32[256,24]{1,0:T(8,128)S(1)} %get-tuple-element.117), kind=kOutput, calls=%fused_computation.35 | convolution fusion | flops 19562496 | bytes 2187264 | tf_op jit(solution)/shard_map/cst,ctd->csd/dot_general | solution.py:23
  145.2 2.7 %copy.57 = bf16[256,24,64]{0,2,1:T(8,128)(2,1)} copy(bf16[256,24,64]{2,1,0:T(8,128)(2,1)} %convolution_convert_fusion) | data formatting | bytes 1572864 | tf_op jit(solution)/shard_map/convert_element_type | solution.py:25
  147.9 3.5 %all-to-all-start.2 = ((bf16[256,4,384]{0,2,1:T(8,128)(2,1)}), bf16[256,4,384]{0,2,1:T(8,128)(2,1)S(1)}, u32[]{:S(2)}, u32[]{:S(2)}) async-start(bf16[256,4,384]{0,2,1:T(8,128)(2,1)} %bitcast.17), calls=%async_computation.2 | async-start | bytes 1572864 | tf_op jit(solution)/shard_map/all_to_all | solution.py:79
  151.5 19.5 %all-to-all-done.2 = bf16[256,4,384]{0,2,1:T(8,128)(2,1)S(1)} async-done(((bf16[256,4,384]{0,2,1:T(8,128)(2,1)}), bf16[256,4,384]{0,2,1:T(8,128)(2,1)S(1)}, u32[]{:S(2)}, u32[]{:S(2)}) %all-to-all-start.2) | async-done | bytes 786464 | tf_op jit(solution)/shard_map/all_to_all | solution.py:79
  173.3 8.5 %while.25 = (s32[]{:T(128)}, bf16[4,768,64]{1,2,0:T(8,128)(2,1)S(1)}, s32[4,768]{1,0:T(4,128)S(1)}, bf16[4,1536,64]{2,1,0:T(8,128)(2,1)}, s32[]{:T(128)}) while((s32[]{:T(128)}, bf16[4,768,64]{1,2,0:T(8,128)(2,1)S(1)}, s32[4,768]{1,0:T(4,128)S(1)}, bf16[4,1536,64]{2,1,0:T(8,128)(2,1)}, s32[]{:T(128)}) %tuple.52), condition=%wide.region_8.9_spmd, body=%wide.region_7.8_spmd.sunk | while | flops 152223744 | bytes 502849 | solution.py:81
  175.5 2.1 fusion.72
  177.6 2.1 fusion.72
  179.7 2.1 fusion.72
  181.8 2.3 fusion.50
  184.1 36.2 %reduce-scatter.2.cloned.1.call-done = f32[768,256]{1,0:T(8,128)} async-done(((f32[768,1024]{1,0:T(8,128)}), f32[768,256]{1,0:T(8,128)}) %reduce-scatter.2.cloned.1.call-update) | async-done | bytes 786448 | tf_op jit(solution)/shard_map/reduce_scatter | solution.py:84
  (71 shorter events, 28.5 us)
Async XLA Ops:
  6.5 175.3 %copy-start = (bf16[256,1024]{1,0:T(8,128)(2,1)S(1)}, bf16[256,1024]{1,0:T(8,128)(2,1)}, u32[]{:S(2)}) copy-start(bf16[256,1024]{1,0:T(8,128)(2,1)} %param.16) | copy-start | bytes 1572868
  6.5 26.9 %copy-start.8 = (f32[1024]{0:T(1024)S(1)}, f32[1024]{0:T(1024)}, u32[]{:S(2)}) copy-start(f32[1024]{0:T(1024)} %param.12) | copy-start | bytes 12292
  6.5 24.9 %all-gather.2.cloned.1.call-start = ((), (), s32[]{:S(2)}) async-start(), calls=%async_computation.4 | async-start | bytes 1966080 | tf_op jit(solution)/shard_map/all_gather | solution.py:52
  31.5 4.3 %copy-start.3 = (bf16[768,1024]{1,0:T(8,128)(2,1)S(1)}, bf16[768,1024]{1,0:T(8,128)(2,1)}, u32[]{:S(2)}) copy-start(bf16[768,1024]{1,0:T(8,128)(2,1)} %all-gather.2.cloned.1.call-done) | copy-start | bytes 4718596
  31.5 4.3 %copy-start.6 = (bf16[1024,256]{1,0:T(8,128)(2,1)S(1)}, bf16[1024,256]{1,0:T(8,128)(2,1)}, u32[]{:S(2)}) copy-start(bf16[1024,256]{1,0:T(8,128)(2,1)} %param.13) | copy-start | bytes 1572868
  35.8 1.0 copy-start.7
  51.5 17.0 %all-to-all-start = ((bf16[1,256,4,6]{1,3,0,2:T(8,128)(2,1)}), bf16[1,256,4,6]{1,3,0,2:T(8,128)(2,1)S(1)}, u32[]{:S(2)}, u32[]{:S(2)}) async-start(bf16[1,256,4,6]{1,3,0,2:T(8,128)(2,1)} %copy.46), calls=%async_computation | async-start | bytes 32768 | tf_op jit(solution)/shard_map/all_to_all | solution.py:76
  68.6 58.8 %all-to-all-start.1 = ((bf16[3,256,4,384]{3,1,0,2:T(8,128)(2,1)}), bf16[3,256,4,384]{3,1,0,2:T(8,128)(2,1)S(1)}, u32[]{:S(2)}, u32[]{:S(2)}) async-start(bf16[3,256,4,384]{3,1,0,2:T(8,128)(2,1)} %copy.49), calls=%async_computation.1 | async-start | bytes 4718592 | tf_op jit(solution)/shard_map/all_to_all | solution.py:75
  128.8 3.3 %copy-start.2 = (bf16[1,256,4,384]{3,1,0,2:T(8,128)(2,1)S(1)}, bf16[1,256,4,384]{3,1,0,2:T(8,128)(2,1)}, u32[]{:S(2)}) copy-start(bf16[1,256,4,384]{3,1,0,2:T(8,128)(2,1)} %get-tuple-element.114) | copy-start | bytes 2359300
  132.1 2.1 copy-start.1
  136.3 4.9 %copy-start.4 = (bf16[256,24,64]{2,1,0:T(8,128)(2,1)S(1)}, bf16[256,24,64]{2,1,0:T(8,128)(2,1)}, u32[]{:S(2)}) copy-start(bf16[256,24,64]{2,1,0:T(8,128)(2,1)} %copy.56) | copy-start | bytes 2359300
  147.9 23.1 %all-to-all-start.2 = ((bf16[256,4,384]{0,2,1:T(8,128)(2,1)}), bf16[256,4,384]{0,2,1:T(8,128)(2,1)S(1)}, u32[]{:S(2)}, u32[]{:S(2)}) async-start(bf16[256,4,384]{0,2,1:T(8,128)(2,1)} %bitcast.17), calls=%async_computation.2 | async-start | bytes 1572864 | tf_op jit(solution)/shard_map/all_to_all | solution.py:79
  151.4 68.9 %reduce-scatter.2.cloned.1.call-start = ((), (), s32[]{:S(2)}) async-start(), calls=%async_computation.5 | async-start | bytes 3932160 | tf_op jit(solution)/shard_map/reduce_scatter | solution.py:84
  184.1 36.3 %copy-start.5 = (bf16[768,256]{1,0:T(8,128)(2,1)S(1)}, bf16[768,256]{1,0:T(8,128)(2,1)}, u32[]{:S(2)}) copy-start(bf16[768,256]{1,0:T(8,128)(2,1)} %param.11) | copy-start | bytes 1179652
Sparse Core Ops, SparseCore 0:
  8.9 22.5 all-gather.1
  184.2 36.0 reduce-scatter.1
where the time goes:
time: 230 us; the launch traced here: 229 us
  waiting for transfers between devices  130 us (57%)
  matrix products  32.2 us (14%)
  local copies, waits for them, and re-layouts  29.2 us (13%)
  between operations  13.6 us (6%)
  starting transfers between devices  13.2 us (6%)
  other arithmetic  10.4 us (5%)
    all_to_all x1, waiting for transfers between devices, on_device(): lax.all_to_all(outgoing, 'seq', split_axis=2, concat_axis=2, tiled=True)  53.5 us
    reduce_scatter x1, waiting for transfers between devices, on_device(): lax.psum_scatter(partial_sums, 'head', scatter_dimension=1, tiled=True)  36.2 us
    all_gather x1, waiting for transfers between devices, on_device(): rows = lax.all_gather(tokens, 'head', axis=1, tiled=True)  20.3 us
    all_to_all x1, waiting for transfers between devices, on_device(): lax.all_to_all(result, 'seq', split_axis=1, concat_axis=1, tiled=True)  19.5 us
    dot_general x4, matrix products, place_head(): jnp.einsum('ts,ctd->csd', onehot, head_parts, preferred_element_type=jnp....  8.72 us
    reshape x2, local copies, waits for them, and re-layouts, on_device(): placed.transpose(1, 0, 2, 3)  8.51 us
    dot_general x4, matrix products, fetch_head(): jnp.dot(onehot, head_back, preferred_element_type=jnp.float32)  8.33 us
    all_to_all x1, starting transfers between devices, on_device(): lax.all_to_all(outgoing, 'seq', split_axis=2, concat_axis=2, tiled=True)  5.09 us
  transfers between devices with their start and end apart: 5, of which 4 were waited for; matrix products, arithmetic and copies ran while one was open for 7% of the time, Pallas kernels for 0%

commit v1 on v0

--- a/solution.py
+++ b/solution.py
@@ -1,6 +1,10 @@
+import functools
+
 import jax
 import jax.numpy as jnp
 from jax import lax
+from jax.experimental import pallas as pl
+from jax.experimental.pallas import tpu as pltpu
 from jax.sharding import PartitionSpec as P
 
 HEAD_DIM = 64
@@ -44,7 +48,7 @@
     return jnp.dot(onehot, head_back, preferred_element_type=jnp.float32).astype(jnp.bfloat16)
 
 
-def on_device(tokens, norm_gain, w_query, w_key, w_value, w_out, cluster_ids):
+def clustered(tokens, norm_gain, w_query, w_key, w_value, w_out, cluster_ids):
     n_seq = lax.axis_size("seq")
     tok = tokens.shape[0]
     heads_here = w_query.shape[1] // HEAD_DIM
@@ -85,6 +89,296 @@
     return (tokens.astype(jnp.float32) + share).astype(jnp.bfloat16)
 
 
+CHUNK = 256
+HALF = CHUNK // 2
+MESH = pl.DeviceIdType.MESH
+LOG2E = 1.4426950408889634
+
+
+def remote(src, dst, send, recv, where):
+    return pltpu.make_async_remote_copy(
+        src_ref=src, dst_ref=dst, send_sem=send, recv_sem=recv, device_id=where, device_id_type=MESH
+    )
+
+
+def layer_kernel(
+    n_seq, n_head, tok_ref, gain_ref, wq_ref, wk_ref, wv_ref, wo_ref, ids_ref, out_ref,
+    xfull, kv_out, kv_in, q_out, q_in, id_in, ret, back, wo_in, w_top, w_bot, sbuf,
+    tok_send, tok_recv, wo_send, wo_recv, id_send, id_recv, kv_send, kv_recv,
+    q_send, q_recv, ret_send, ret_recv, rl_send, rl_recv,
+):
+    s = lax.axis_index("seq")
+    h = lax.axis_index("head")
+    tok, width = tok_ref.shape
+    chunks = tok // CHUNK
+    sib = h + 1 - 2 * lax.rem(h, 2)
+    par = lax.rem(h + 2, 4)
+    dia = lax.rem(sib + 2, 4)
+    seq_at = [lax.rem(s + i, n_seq) for i in range(n_seq)]
+    seq_from = [lax.rem(s + n_seq - i, n_seq) for i in range(n_seq)]
+    head_at = [lax.rem(h + j, n_head) for j in range(n_head)]
+    head_from = [lax.rem(h + n_head - j, n_head) for j in range(n_head)]
+
+    barrier = pltpu.get_barrier_semaphore()
+    for i in range(1, n_seq):
+        pl.semaphore_signal(barrier, inc=1, device_id={"seq": seq_at[i]}, device_id_type=MESH)
+    for j in range(1, n_head):
+        pl.semaphore_signal(barrier, inc=1, device_id={"head": head_at[j]}, device_id_type=MESH)
+    pl.semaphore_wait(barrier, n_seq + n_head - 2)
+
+    def rows(c):
+        return pl.ds(pl.multiple_of(c * CHUNK, CHUNK), CHUNK)
+
+    def packed(c):
+        return pl.ds(pl.multiple_of(c * HALF, HALF), HALF)
+
+    started = []
+
+    def tok_copy(kind, c, owner, to):
+        src = tok_ref.at[rows(c)] if kind < 2 else xfull.at[owner, rows(c)]
+        return remote(src, xfull.at[owner, rows(c)], tok_send.at[kind, c], tok_recv.at[kind, c], {"head": to})
+
+    for c in range(chunks):
+        for kind, to in ((0, par), (1, sib)):
+            copy = tok_copy(kind, c, h, to)
+            copy.start()
+            started.append(copy)
+    for i in range(1, n_seq):
+        copy = remote(ids_ref.at[seq_at[i]], id_in.at[s], id_send.at[i], id_recv.at[i], {"seq": seq_at[i]})
+        copy.start()
+        started.append(copy)
+    for j in range(1, n_head):
+        cols = pl.ds(pl.multiple_of(head_at[j] * width, width), width)
+        copy = remote(wo_ref.at[:, cols], wo_in.at[h], wo_send.at[j], wo_recv.at[j], {"head": head_at[j]})
+        copy.start()
+        started.append(copy)
+    xfull[h] = tok_ref[...]
+    id_in[s] = ids_ref[s]
+    wo_in[h] = wo_ref[:, pl.ds(pl.multiple_of(h * width, width), width)]
+    w_top[...] = jnp.zeros_like(w_top)
+    w_bot[...] = jnp.zeros_like(w_bot)
+
+    lane = lax.broadcasted_iota(jnp.int32, (HALF, 2 * HEAD_DIM), 1)
+    low = lane < HEAD_DIM
+
+    for c in range(chunks):
+        tok_copy(0, c, par, par).wait_recv()
+        copy = tok_copy(2, c, par, sib)
+        copy.start()
+        started.append(copy)
+        tok_copy(1, c, sib, sib).wait_recv()
+        tok_copy(2, c, dia, sib).wait_recv()
+        here = pl.ds(c * CHUNK, CHUNK)
+        x = jnp.concatenate([xfull[g, here].astype(jnp.float32) for g in range(n_head)], axis=1)
+        square = jnp.sum(x * x, axis=1, keepdims=True) * (1.0 / x.shape[1])
+        normed = (x * lax.rsqrt(square + 1e-05) * gain_ref[...]).astype(jnp.bfloat16)
+        k = jnp.dot(normed, wk_ref[...], preferred_element_type=jnp.float32)
+        v = jnp.dot(normed, wv_ref[...], preferred_element_type=jnp.float32)
+        for t in range(n_seq):
+            cols = slice(t * HEAD_DIM, (t + 1) * HEAD_DIM)
+            kv_out[t, here] = jnp.concatenate([k[:, cols], v[:, cols]], axis=1).astype(jnp.bfloat16)
+        for i in range(1, n_seq):
+            copy = remote(
+                kv_out.at[seq_at[i], here], kv_in.at[s, here],
+                kv_send.at[i, c], kv_recv.at[i, c], {"seq": seq_at[i]},
+            )
+            copy.start()
+            started.append(copy)
+        kv_in[s, here] = kv_out[s, here]
+        q = jnp.dot(normed, wq_ref[...], preferred_element_type=jnp.float32)
+        pack = pl.ds(c * HALF, HALF)
+        for t in range(n_seq):
+            cols = slice(t * HEAD_DIM, (t + 1) * HEAD_DIM)
+            q_out[t, pack] = jnp.concatenate([q[:HALF, cols], q[HALF:, cols]], axis=1).astype(jnp.bfloat16)
+    for c in range(chunks):
+        pack = pl.ds(c * HALF, HALF)
+        for i in range(1, n_seq):
+            copy = remote(
+                q_out.at[seq_at[i], pack], q_in.at[s, pack],
+                q_send.at[i, c], q_recv.at[i, c], {"seq": seq_at[i]},
+            )
+            copy.start()
+            started.append(copy)
+    q_in[s] = q_out[s]
+
+    for j in range(1, n_head):
+        remote(
+            wo_ref.at[:, pl.ds(0, width)], wo_in.at[head_from[j]], wo_send.at[j], wo_recv.at[j],
+            {"head": head_from[j]},
+        ).wait_recv()
+    for g in range(n_head):
+        for t in range(n_seq):
+            part = wo_in[g, t * HEAD_DIM:(t + 1) * HEAD_DIM, :]
+            at = (g * n_seq + t) * 2 * HEAD_DIM
+            w_top[at:at + HEAD_DIM, :] = part
+            w_bot[at + HEAD_DIM:at + 2 * HEAD_DIM, :] = part
+    for i in range(1, n_seq):
+        remote(
+            ids_ref.at[seq_from[i]], id_in.at[seq_from[i]], id_send.at[i], id_recv.at[i],
+            {"seq": seq_from[i]},
+        ).wait_recv()
+    for c in range(chunks):
+        for i in range(1, n_seq):
+            here = pl.ds(c * CHUNK, CHUNK)
+            remote(
+                kv_out.at[seq_from[i], here], kv_in.at[seq_from[i], here],
+                kv_send.at[i, c], kv_recv.at[i, c], {"seq": seq_from[i]},
+            ).wait_recv()
+
+    def attend(source, c):
+        pair = q_in[source, packed(c)].astype(jnp.float32)
+        turned = pltpu.roll(pair, HEAD_DIM, 1)
+        query = jnp.concatenate(
+            [jnp.where(low, pair, 0.0), jnp.where(low, turned, 0.0)], axis=0
+        ).astype(jnp.bfloat16)
+        own = jnp.broadcast_to(id_in[source, c, 0:1, :], (CHUNK, CHUNK)).T
+        top = None
+        for block in range(n_seq * chunks):
+            j, e = block // chunks, block % chunks
+            kv = kv_in[j, e * CHUNK:(e + 1) * CHUNK, :]
+            score = lax.dot_general(query, kv, (((1,), (1,)), ((), ())), preferred_element_type=jnp.float32)
+            score = jnp.where(own == id_in[j, e, 0:1, :], score, jnp.float32(-1e30))
+            sbuf[:, block * CHUNK:(block + 1) * CHUNK] = score
+            peak = jnp.maximum(score[:, :HALF], score[:, HALF:])
+            top = peak if top is None else jnp.maximum(top, peak)
+        top = jnp.max(top, axis=1, keepdims=True)
+        total = None
+        acc = None
+        for block in range(n_seq * chunks):
+            j, e = block // chunks, block % chunks
+            kv = kv_in[j, e * CHUNK:(e + 1) * CHUNK, :]
+            score = sbuf[:, block * CHUNK:(block + 1) * CHUNK]
+            expo = jnp.exp2((score - top) * jnp.float32(LOG2E * HEAD_DIM ** -0.5))
+            summed = expo[:, :HALF] + expo[:, HALF:]
+            total = summed if total is None else total + summed
+            term = jnp.dot(expo.astype(jnp.bfloat16), kv, preferred_element_type=jnp.float32)
+            acc = term if acc is None else acc + term
+        result = acc / jnp.sum(total, axis=1, keepdims=True)
+        return jnp.where(low, pltpu.roll(result[:HALF], HEAD_DIM, 1), result[HALF:]).astype(jnp.bfloat16)
+
+    def ret_copy(i, c, slot, to):
+        return remote(
+            ret.at[i, packed(c)], back.at[h, slot, packed(c)],
+            ret_send.at[i, c], ret_recv.at[i, c], {"seq": to},
+        )
+
+    def relay(i, c, j, owner, to):
+        slot = lax.rem(s + n_seq - i, n_seq)
+        return remote(
+            back.at[owner, slot, packed(c)], back.at[owner, slot, packed(c)],
+            rl_send.at[j, i, c], rl_recv.at[j, i, c], {"head": to},
+        )
+
+    def pass_on(i, c):
+        for j in range(1, n_head):
+            relay(i, c, j, h, head_at[j]).start()
+
+    def back_wait(i, c):
+        sender = lax.rem(s + n_seq - i, n_seq)
+        ret_copy(i, c, sender, sender).wait_recv()
+
+    @pl.loop(0, n_seq)
+    def _(i):
+        source = lax.rem(s + i, n_seq)
+
+        @pl.loop(0, chunks)
+        def _(c):
+            @pl.when(i > 0)
+            def _():
+                remote(
+                    q_out.at[source, packed(c)], q_in.at[source, packed(c)],
+                    q_send.at[n_seq - i, c], q_recv.at[n_seq - i, c], {"seq": source},
+                ).wait_recv()
+
+            result = attend(source, c)
+
+            @pl.when(i == 0)
+            def _():
+                back[h, s, packed(c)] = result
+                pass_on(0, c)
+
+            @pl.when(i > 0)
+            def _():
+                ret[i, packed(c)] = result
+                ret_copy(i, c, s, source).start()
+
+            @pl.when(i > 1)
+            def _():
+                back_wait(i - 1, c)
+                pass_on(i - 1, c)
+
+    for c in range(chunks):
+        back_wait(n_seq - 1, c)
+        pass_on(n_seq - 1, c)
+    for c in range(chunks):
+        for i in range(n_seq):
+            for j in range(1, n_head):
+                relay(i, c, j, head_from[j], head_from[j]).wait_recv()
+        pack = pl.ds(c * HALF, HALF)
+        mixed = jnp.concatenate([back[g, t, pack] for g in range(n_head) for t in range(n_seq)], axis=1)
+        for weight, at in ((w_top, c * CHUNK), (w_bot, c * CHUNK + HALF)):
+            branch = jnp.dot(mixed, weight[...], preferred_element_type=jnp.float32)
+            out_ref[at:at + HALF, :] = (tok_ref[at:at + HALF, :].astype(jnp.float32) + branch).astype(jnp.bfloat16)
+    for copy in started:
+        copy.wait_send()
+    for c in range(chunks):
+        for i in range(n_seq):
+            if i > 0:
+                ret_copy(i, c, s, seq_at[i]).wait_send()
+            for j in range(1, n_head):
+                relay(i, c, j, h, head_at[j]).wait_send()
+
+
+def dense(tokens, norm_gain, w_query, w_key, w_value, w_out, cluster_ids):
+    n_seq, n_head = lax.axis_size("seq"), lax.axis_size("head")
+    tok, width = tokens.shape
+    chunks = tok // CHUNK
+    ids = cluster_ids[:, :, 0].astype(jnp.float32).reshape(n_seq, chunks, 1, CHUNK)
+    ids = jnp.broadcast_to(ids, (n_seq, chunks, 8, CHUNK))
+    pair = 2 * HEAD_DIM
+    bf16, f32 = jnp.bfloat16, jnp.float32
+    vmem, dma = pltpu.VMEM, pltpu.SemaphoreType.DMA
+    return pl.pallas_call(
+        functools.partial(layer_kernel, n_seq, n_head),
+        out_shape=jax.ShapeDtypeStruct((tok, width), bf16),
+        in_specs=[pl.BlockSpec(memory_space=pltpu.VMEM)] * 7,
+        out_specs=pl.BlockSpec(memory_space=pltpu.VMEM),
+        scratch_shapes=[
+            vmem((n_head, tok, width), bf16),
+            vmem((n_seq, tok, pair), bf16),
+            vmem((n_seq, tok, pair), bf16),
+            vmem((n_seq, tok // 2, pair), bf16),
+            vmem((n_seq, tok // 2, pair), bf16),
+            vmem((n_seq, chunks, 8, CHUNK), f32),
+            vmem((n_seq, tok // 2, pair), bf16),
+            vmem((n_head, n_seq, tok // 2, pair), bf16),
+            vmem((n_head, width, width), bf16),
+            vmem((n_head * n_seq * pair, width), bf16),
+            vmem((n_head * n_seq * pair, width), bf16),
+            vmem((CHUNK, n_seq * tok), f32),
+            dma((3, chunks)), dma((3, chunks)),
+            dma((n_head,)), dma((n_head,)),
+            dma((n_seq,)), dma((n_seq,)),
+            dma((n_seq, chunks)), dma((n_seq, chunks)),
+            dma((n_seq, chunks)), dma((n_seq, chunks)),
+            dma((n_seq, chunks)), dma((n_seq, chunks)),
+            dma((n_head, n_seq, chunks)), dma((n_head, n_seq, chunks)),
+        ],
+        compiler_params=pltpu.CompilerParams(
+            collective_id=0, has_side_effects=True, vmem_limit_bytes=48 * 1024 * 1024
+        ),
+    )(tokens, norm_gain.reshape(1, -1), w_query, w_key, w_value, w_out, ids)
+
+
+def on_device(*operands):
+    tokens, w_query = operands[0], operands[2]
+    n_seq, n_head = lax.axis_size("seq"), lax.axis_size("head")
+    heads_here = w_query.shape[1] // HEAD_DIM
+    if n_head == 4 and heads_here == n_seq and tokens.shape[0] % CHUNK == 0 and n_seq > 1:
+        return dense(*operands)
+    return clustered(*operands)
+
+
 def solution(mesh):
     return jax.shard_map(
         on_device,

time: 230 us -> 73.4 us (0.32)
  waiting for transfers between devices: 130 us -> 0 us
  Pallas kernels: 0 us -> 65.6 us
  matrix products: 32.2 us -> 0 us
  local copies, waits for them, and re-layouts: 29.2 us -> 6.59 us
  between operations: 13.6 us -> 0.05 us
  starting transfers between devices: 13.2 us -> 0 us
  other arithmetic: 10.4 us -> 0.72 us
    all_to_all x3 -> x0, waiting for transfers between devices: 73 us -> none  [the longest x1 53.5 us: on_device(): lax.all_to_all(outgoing, 'seq', split_axis=2, concat_axis=2, tiled=True)]
    pallas_call x0 -> x1, Pallas kernels: none -> 65.6 us  [dense(): pl.pallas_call(functools.partial(layer_kernel, n_seq, n_head), out_shape=...]
    reduce_scatter x1 -> x0, waiting for transfers between devices: 36.2 us -> none  [on_device(): lax.psum_scatter(partial_sums, 'head', scatter_dimension=1, tiled=True)]
    dot_general x13 -> x0, matrix products: 27.3 us -> none  [the longest x4 8.72 us: place_head(): jnp.einsum('ts,ctd->csd', onehot, head_parts, preferred_element_type=jnp....]
    all_gather x1 -> x0, waiting for transfers between devices: 20.3 us -> none  [on_device(): rows = lax.all_gather(tokens, 'head', axis=1, tiled=True)]
    all_to_all x3 -> x0, starting transfers between devices: 13.2 us -> none  [the longest x1 5.09 us: on_device(): lax.all_to_all(outgoing, 'seq', split_axis=2, concat_axis=2, tiled=True)]
    reshape x5 -> x0, local copies, waits for them, and re-layouts: 11.5 us -> none  [the longest x2 8.51 us: on_device(): placed.transpose(1, 0, 2, 3)]
    reduce_sum x6 -> x0, other arithmetic: 6.33 us -> none  [the longest x1 2.23 us: on_device(): rank = jnp.sum(same.astype(jnp.int32), axis=2)]
  transfers between devices with their start and end apart: 5 -> 0, of which waited for: 4 -> 0; matrix products, arithmetic and copies ran while one was open for 7% -> 0% of each run, Pallas kernels for 0% -> 0%
where the time goes in v1:
time: 73.4 us; the launch traced here: 73 us
  Pallas kernels  65.6 us (89%)
  local copies, waits for them, and re-layouts  6.59 us (9%)
    pallas_call x1, Pallas kernels, dense(): pl.pallas_call(functools.partial(layer_kernel, n_seq, n_head), out_shape=...  65.6 us
    unnamed x13, local copies, waits for them, and re-layouts  6.57 us

profile of v1, /device:TPU:0, one launch (start us, length us, event | category | flops | bytes accessed | tf_op | source)
XLA Modules:
  0.0 73.0 jit_solution(11795400209703474629)
XLA Ops:
  0.0 0.7 convert_element_type.10
  0.7 0.0 copy-start.5
  0.8 0.7 copy-done.5
  1.4 0.0 copy-start
  1.4 1.0 %copy-done = bf16[1024,256]{1,0:T(8,128)(2,1)S(1)} copy-done((bf16[1024,256]{1,0:T(8,128)(2,1)S(1)}, bf16[1024,256]{1,0:T(8,128)(2,1)}, u32[]{:S(2)}) %copy-start) | copy-done | bytes 524312
  2.5 0.0 copy-start.1
  2.5 1.0 %copy-done.1 = bf16[1024,256]{1,0:T(8,128)(2,1)S(1)} copy-done((bf16[1024,256]{1,0:T(8,128)(2,1)S(1)}, bf16[1024,256]{1,0:T(8,128)(2,1)}, u32[]{:S(2)}) %copy-start.1) | copy-done | bytes 524312
  3.5 0.0 copy-start.2
  3.5 1.0 %copy-done.2 = bf16[1024,256]{1,0:T(8,128)(2,1)S(1)} copy-done((bf16[1024,256]{1,0:T(8,128)(2,1)S(1)}, bf16[1024,256]{1,0:T(8,128)(2,1)}, u32[]{:S(2)}) %copy-start.2) | copy-done | bytes 524312
  4.6 0.0 copy-start.3
  4.6 1.0 %copy-done.3 = bf16[256,1024]{1,0:T(8,128)(2,1)S(1)} copy-done((bf16[256,1024]{1,0:T(8,128)(2,1)S(1)}, bf16[256,1024]{1,0:T(8,128)(2,1)}, u32[]{:S(2)}) %copy-start.3) | copy-done | bytes 524312
  5.6 0.0 copy-start.4
  5.6 1.0 %copy-done.4 = bf16[768,256]{1,0:T(8,128)(2,1)S(1)} copy-done((bf16[768,256]{1,0:T(8,128)(2,1)S(1)}, bf16[768,256]{1,0:T(8,128)(2,1)}, u32[]{:S(2)}) %copy-start.4) | copy-done | bytes 393240
  6.6 65.6 %shard_map.73 = bf16[768,256]{1,0:T(8,128)(2,1)S(1)} custom-call(bf16[768,256]{1,0:T(8,128)(2,1)S(1)} %copy-done.4, f32[1,1024]{1,0:T(1,128)S(1)} %bitcast.2, bf16[1024,256]{1,0:T(8,128)(2,1)S(1)} %copy-done, bf16[1024,256]{1,0:T(8,128)(2,1)S(1)} %copy-done.1, bf16[1024,256]{1,0:T(8,128)(2,1)S(1)} %copy-done.2, bf16[256,1024]{1,0:T(8,128)(2,1)S(1)} %copy-done.3, ...), custom_call_target="tpu_custom_call" | custom-call | tf_op jit(solution)/shard_map/pallas_call | solution.py:341
  72.2 0.7 %copy.11 = bf16[768,256]{1,0:T(8,128)(2,1)} copy(bf16[768,256]{1,0:T(8,128)(2,1)S(1)} %shard_map.73) | data formatting | bytes 786432
  (3 shorter events, 0.0 us)
Async XLA Ops:
  0.7 0.7 copy-start.5
  1.4 1.0 %copy-start = (bf16[1024,256]{1,0:T(8,128)(2,1)S(1)}, bf16[1024,256]{1,0:T(8,128)(2,1)}, u32[]{:S(2)}) copy-start(bf16[1024,256]{1,0:T(8,128)(2,1)} %wq_ref.1) | copy-start | bytes 1572868
  2.5 1.0 %copy-start.1 = (bf16[1024,256]{1,0:T(8,128)(2,1)S(1)}, bf16[1024,256]{1,0:T(8,128)(2,1)}, u32[]{:S(2)}) copy-start(bf16[1024,256]{1,0:T(8,128)(2,1)} %wk_ref.1) | copy-start | bytes 1572868
  3.5 1.0 %copy-start.2 = (bf16[1024,256]{1,0:T(8,128)(2,1)S(1)}, bf16[1024,256]{1,0:T(8,128)(2,1)}, u32[]{:S(2)}) copy-start(bf16[1024,256]{1,0:T(8,128)(2,1)} %wv_ref.1) | copy-start | bytes 1572868
  4.6 1.0 %copy-start.3 = (bf16[256,1024]{1,0:T(8,128)(2,1)S(1)}, bf16[256,1024]{1,0:T(8,128)(2,1)}, u32[]{:S(2)}) copy-start(bf16[256,1024]{1,0:T(8,128)(2,1)} %wo_ref.1) | copy-start | bytes 1572868
  5.6 1.0 %copy-start.4 = (bf16[768,256]{1,0:T(8,128)(2,1)S(1)}, bf16[768,256]{1,0:T(8,128)(2,1)}, u32[]{:S(2)}) copy-start(bf16[768,256]{1,0:T(8,128)(2,1)} %tok_ref.1) | copy-start | bytes 1179652

commit v2 on v1

--- a/solution.py
+++ b/solution.py
@@ -102,7 +102,8 @@
 
 
 def layer_kernel(
-    n_seq, n_head, tok_ref, gain_ref, wq_ref, wk_ref, wv_ref, wo_ref, ids_ref, out_ref,
+    n_seq, n_head, tok_ref, gain_hbm, wq_hbm, wk_hbm, wv_hbm, wo_ref, ids_ref, out_ref,
+    gain_ref, wq_ref, wk_ref, wv_ref, load_sem,
     xfull, kv_out, kv_in, q_out, q_in, id_in, ret, back, wo_in, w_top, w_bot, sbuf,
     tok_send, tok_recv, wo_send, wo_recv, id_send, id_recv, kv_send, kv_recv,
     q_send, q_recv, ret_send, ret_recv, rl_send, rl_recv,
@@ -119,6 +120,16 @@
     head_at = [lax.rem(h + j, n_head) for j in range(n_head)]
     head_from = [lax.rem(h + n_head - j, n_head) for j in range(n_head)]
 
+    own_cols = pl.ds(pl.multiple_of(h * width, width), width)
+    loads = [
+        pltpu.make_async_copy(src, dst, load_sem.at[n])
+        for n, (src, dst) in enumerate((
+            (tok_ref, xfull.at[h]), (gain_hbm, gain_ref), (wk_hbm, wk_ref), (wv_hbm, wv_ref), (wq_hbm, wq_ref),
+            (wo_ref.at[:, own_cols], wo_in.at[h]), (ids_ref.at[s], id_in.at[s]),
+        ))
+    ]
+    for load in loads:
+        load.start()
     barrier = pltpu.get_barrier_semaphore()
     for i in range(1, n_seq):
         pl.semaphore_signal(barrier, inc=1, device_id={"seq": seq_at[i]}, device_id_type=MESH)
@@ -147,20 +158,24 @@
         copy = remote(ids_ref.at[seq_at[i]], id_in.at[s], id_send.at[i], id_recv.at[i], {"seq": seq_at[i]})
         copy.start()
         started.append(copy)
-    for j in range(1, n_head):
-        cols = pl.ds(pl.multiple_of(head_at[j] * width, width), width)
-        copy = remote(wo_ref.at[:, cols], wo_in.at[h], wo_send.at[j], wo_recv.at[j], {"head": head_at[j]})
-        copy.start()
-        started.append(copy)
-    xfull[h] = tok_ref[...]
-    id_in[s] = ids_ref[s]
-    wo_in[h] = wo_ref[:, pl.ds(pl.multiple_of(h * width, width), width)]
     w_top[...] = jnp.zeros_like(w_top)
     w_bot[...] = jnp.zeros_like(w_bot)
 
+    def query_copy(i, c):
+        return remote(
+            q_out.at[lax.rem(s + i, n_seq), packed(c)], q_in.at[s, packed(c)],
+            q_send.at[i, c], q_recv.at[i, c], {"seq": lax.rem(s + i, n_seq)},
+        )
+
+    def send_queries(i):
+        for c in range(chunks):
+            query_copy(i, c).start()
+
     lane = lax.broadcasted_iota(jnp.int32, (HALF, 2 * HEAD_DIM), 1)
     low = lane < HEAD_DIM
 
+    for load in loads:
+        load.wait()
     for c in range(chunks):
         tok_copy(0, c, par, par).wait_recv()
         copy = tok_copy(2, c, par, sib)
@@ -190,17 +205,11 @@
         for t in range(n_seq):
             cols = slice(t * HEAD_DIM, (t + 1) * HEAD_DIM)
             q_out[t, pack] = jnp.concatenate([q[:HALF, cols], q[HALF:, cols]], axis=1).astype(jnp.bfloat16)
-    for c in range(chunks):
-        pack = pl.ds(c * HALF, HALF)
-        for i in range(1, n_seq):
-            copy = remote(
-                q_out.at[seq_at[i], pack], q_in.at[s, pack],
-                q_send.at[i, c], q_recv.at[i, c], {"seq": seq_at[i]},
-            )
-            copy.start()
-            started.append(copy)
-    q_in[s] = q_out[s]
-
+    for j in range(1, n_head):
+        cols = pl.ds(pl.multiple_of(head_at[j] * width, width), width)
+        copy = remote(wo_ref.at[:, cols], wo_in.at[h], wo_send.at[j], wo_recv.at[j], {"head": head_at[j]})
+        copy.start()
+        started.append(copy)
     for j in range(1, n_head):
         remote(
             wo_ref.at[:, pl.ds(0, width)], wo_in.at[head_from[j]], wo_send.at[j], wo_recv.at[j],
@@ -224,6 +233,9 @@
                 kv_out.at[seq_from[i], here], kv_in.at[seq_from[i], here],
                 kv_send.at[i, c], kv_recv.at[i, c], {"seq": seq_from[i]},
             ).wait_recv()
+
+    send_queries(n_seq - 1)
+    q_in[s] = q_out[s]
 
     def attend(source, c):
         pair = q_in[source, packed(c)].astype(jnp.float32)
@@ -262,71 +274,99 @@
             ret_send.at[i, c], ret_recv.at[i, c], {"seq": to},
         )
 
-    def relay(i, c, j, owner, to):
-        slot = lax.rem(s + n_seq - i, n_seq)
-        return remote(
-            back.at[owner, slot, packed(c)], back.at[owner, slot, packed(c)],
-            rl_send.at[j, i, c], rl_recv.at[j, i, c], {"head": to},
-        )
+    def relay(kind, i, c, owner, to):
+        part = back.at[owner, lax.rem(s + n_seq - i, n_seq), packed(c)]
+        return remote(part, part, rl_send.at[kind, i, c], rl_recv.at[kind, i, c], {"head": to})
 
     def pass_on(i, c):
-        for j in range(1, n_head):
-            relay(i, c, j, h, head_at[j]).start()
+        relay(0, i, c, h, par).start()
+        relay(1, i, c, h, sib).start()
+
+    def forward(i, c):
+        relay(0, i, c, par, par).wait_recv()
+        relay(2, i, c, par, sib).start()
 
     def back_wait(i, c):
         sender = lax.rem(s + n_seq - i, n_seq)
         ret_copy(i, c, sender, sender).wait_recv()
 
-    @pl.loop(0, n_seq)
-    def _(i):
+    lead = chunks - 1
+    distant = (n_seq - 1) * chunks
+    lag = 2
+
+    @pl.loop(0, n_seq * chunks)
+    def _(n):
+        r = n - lead
+        is_own = (n < lead) | (n == n_seq * chunks - 1)
+        i = jnp.where(is_own, 0, (r + chunks) // chunks)
+        c = jnp.where(n < lead, n, jnp.where(is_own, chunks - 1, lax.rem(r + chunks, chunks)))
         source = lax.rem(s + i, n_seq)
 
-        @pl.loop(0, chunks)
-        def _(c):
-            @pl.when(i > 0)
-            def _():
-                remote(
-                    q_out.at[source, packed(c)], q_in.at[source, packed(c)],
-                    q_send.at[n_seq - i, c], q_recv.at[n_seq - i, c], {"seq": source},
-                ).wait_recv()
-
-            result = attend(source, c)
-
-            @pl.when(i == 0)
-            def _():
-                back[h, s, packed(c)] = result
-                pass_on(0, c)
-
-            @pl.when(i > 0)
-            def _():
-                ret[i, packed(c)] = result
-                ret_copy(i, c, s, source).start()
-
-            @pl.when(i > 1)
-            def _():
-                back_wait(i - 1, c)
-                pass_on(i - 1, c)
-
-    for c in range(chunks):
-        back_wait(n_seq - 1, c)
-        pass_on(n_seq - 1, c)
+        for step in range(2, n_seq):
+            @pl.when(n == 2 * (step - 2) + 1)
+            def _(step=step):
+                send_queries(n_seq - step)
+
+        @pl.when(i > 0)
+        def _():
+            remote(
+                q_out.at[source, packed(c)], q_in.at[source, packed(c)],
+                q_send.at[n_seq - i, c], q_recv.at[n_seq - i, c], {"seq": source},
+            ).wait_recv()
+
+        result = attend(source, c)
+
+        @pl.when(i == 0)
+        def _():
+            back[h, s, packed(c)] = result
+            pass_on(0, c)
+
+        @pl.when(i > 0)
+        def _():
+            ret[i, packed(c)] = result
+            ret_copy(i, c, s, source).start()
+
+        @pl.when((r >= 0) & (r < lead))
+        def _():
+            forward(0, r)
+
+        @pl.when(r >= lag)
+        def _():
+            e = r - lag
+            back_wait(e // chunks + 1, lax.rem(e, chunks))
+            pass_on(e // chunks + 1, lax.rem(e, chunks))
+
+        @pl.when(r >= 2 * lag)
+        def _():
+            e = r - 2 * lag
+            forward(e // chunks + 1, lax.rem(e, chunks))
+
+    for e in range(distant + 1 - lag, distant):
+        back_wait(e // chunks + 1, e % chunks)
+        pass_on(e // chunks + 1, e % chunks)
+    for e in range(distant + 1 - 2 * lag, distant - 1):
+        forward(e // chunks + 1, e % chunks)
+    forward(0, chunks - 1)
+    forward(n_seq - 1, chunks - 1)
     for c in range(chunks):
         for i in range(n_seq):
-            for j in range(1, n_head):
-                relay(i, c, j, head_from[j], head_from[j]).wait_recv()
+            relay(1, i, c, sib, sib).wait_recv()
+            relay(2, i, c, dia, sib).wait_recv()
         pack = pl.ds(c * HALF, HALF)
         mixed = jnp.concatenate([back[g, t, pack] for g in range(n_head) for t in range(n_seq)], axis=1)
         for weight, at in ((w_top, c * CHUNK), (w_bot, c * CHUNK + HALF)):
             branch = jnp.dot(mixed, weight[...], preferred_element_type=jnp.float32)
-            out_ref[at:at + HALF, :] = (tok_ref[at:at + HALF, :].astype(jnp.float32) + branch).astype(jnp.bfloat16)
+            out_ref[at:at + HALF, :] = (xfull[h, at:at + HALF, :].astype(jnp.float32) + branch).astype(jnp.bfloat16)
     for copy in started:
         copy.wait_send()
     for c in range(chunks):
         for i in range(n_seq):
             if i > 0:
+                query_copy(i, c).wait_send()
                 ret_copy(i, c, s, seq_at[i]).wait_send()
-            for j in range(1, n_head):
-                relay(i, c, j, h, head_at[j]).wait_send()
+            relay(0, i, c, h, par).wait_send()
+            relay(1, i, c, h, sib).wait_send()
+            relay(2, i, c, par, sib).wait_send()
 
 
 def dense(tokens, norm_gain, w_query, w_key, w_value, w_out, cluster_ids):
@@ -341,9 +381,12 @@
     return pl.pallas_call(
         functools.partial(layer_kernel, n_seq, n_head),
         out_shape=jax.ShapeDtypeStruct((tok, width), bf16),
-        in_specs=[pl.BlockSpec(memory_space=pltpu.VMEM)] * 7,
+        in_specs=[pl.BlockSpec(memory_space=pltpu.HBM)] * 7,
         out_specs=pl.BlockSpec(memory_space=pltpu.VMEM),
         scratch_shapes=[
+            vmem((1, n_head * width), f32),
+            vmem(w_query.shape, bf16), vmem(w_query.shape, bf16), vmem(w_query.shape, bf16),
+            dma((7,)),
             vmem((n_head, tok, width), bf16),
             vmem((n_seq, tok, pair), bf16),
             vmem((n_seq, tok, pair), bf16),
@@ -362,10 +405,10 @@
             dma((n_seq, chunks)), dma((n_seq, chunks)),
             dma((n_seq, chunks)), dma((n_seq, chunks)),
             dma((n_seq, chunks)), dma((n_seq, chunks)),
-            dma((n_head, n_seq, chunks)), dma((n_head, n_seq, chunks)),
+            dma((3, n_seq, chunks)), dma((3, n_seq, chunks)),
         ],
         compiler_params=pltpu.CompilerParams(
-            collective_id=0, has_side_effects=True, vmem_limit_bytes=48 * 1024 * 1024
+            collective_id=0, has_side_effects=True, vmem_limit_bytes=60 * 1024 * 1024
         ),
     )(tokens, norm_gain.reshape(1, -1), w_query, w_key, w_value, w_out, ids)
 

time: 73.4 us -> 65.6 us (0.89)
  local copies, waits for them, and re-layouts: 6.59 us -> 2.43 us
  Pallas kernels: 65.6 us -> 62.3 us
    unnamed x13 -> x1, local copies, waits for them, and re-layouts: 6.57 us -> 1.77 us
    pallas_call x1, Pallas kernels: 65.6 us -> 62.3 us  [dense(): pl.pallas_call(functools.partial(layer_kernel, n_seq, n_head), out_shape=...]
where the time goes in v2:
time: 65.6 us; the launch traced here: 65.4 us
  Pallas kernels  62.3 us (95%)
  local copies, waits for them, and re-layouts  2.43 us (4%)
  other arithmetic  0.72 us (1%)
    pallas_call x1, Pallas kernels, dense(): pl.pallas_call(functools.partial(layer_kernel, n_seq, n_head), out_shape=...  62.3 us
    unnamed x1, local copies, waits for them, and re-layouts  1.77 us

profile of v2, /device:TPU:0, one launch (start us, length us, event | category | flops | bytes accessed | tf_op | source)
XLA Modules:
  0.0 65.4 jit_solution(12275105039775016784)
XLA Ops:
  0.0 0.7 %convert_element_type.10 = f32[4,768,1]{1,2,0:T(1,128)S(1)} convert(s32[4,768,1]{1,2,0:T(1,128)} %param.13) | non-fusion elementwise | flops 3072 | bytes 24576 | tf_op jit(solution)/shard_map/convert_element_type | solution.py:376
  0.7 0.6 broadcast_in_dim.2.ids_ref
  1.4 62.3 %shard_map.73 = bf16[768,256]{1,0:T(8,128)(2,1)} custom-call(bf16[768,256]{1,0:T(8,128)(2,1)} %tok_ref.1, f32[1,1024]{1,0:T(1,128)} %bitcast.3, bf16[1024,256]{1,0:T(8,128)(2,1)} %wq_hbm.1, bf16[1024,256]{1,0:T(8,128)(2,1)} %wk_hbm.1, bf16[1024,256]{1,0:T(8,128)(2,1)} %wv_hbm.1, bf16[256,1024]{1,0:T(8,128)(2,1)} %wo_ref.1, ...), custom_call_target="tpu_custom_call" | custom-call | tf_op jit(solution)/shard_map/pallas_call | solution.py:381
  63.7 1.8 %copy.11 = bf16[768,256]{1,0:T(8,128)(2,1)} copy(bf16[768,256]{1,0:T(8,128)(2,1)} %shard_map.73) | data formatting | bytes 786432
  (2 shorter events, 0.0 us)

commit v3 on v2

--- a/solution.py
+++ b/solution.py
@@ -292,7 +292,7 @@
 
     lead = chunks - 1
     distant = (n_seq - 1) * chunks
-    lag = 2
+    lag = 3
 
     @pl.loop(0, n_seq * chunks)
     def _(n):

time: 65.6 us -> 65.2 us (level)
  no operation moved by 1% of the time
where the time goes in v3:
time: 65.2 us; the launch traced here: 65 us
  Pallas kernels  61.9 us (95%)
  local copies, waits for them, and re-layouts  2.43 us (4%)
  other arithmetic  0.72 us (1%)
    pallas_call x1, Pallas kernels, dense(): pl.pallas_call(functools.partial(layer_kernel, n_seq, n_head), out_shape=...  61.9 us
    unnamed x1, local copies, waits for them, and re-layouts  1.77 us

profile of v3, /device:TPU:0, one launch (start us, length us, event | category | flops | bytes accessed | tf_op | source)
XLA Modules:
  0.0 65.0 jit_solution(17214571127582556839)
XLA Ops:
  0.0 0.7 %convert_element_type.10 = f32[4,768,1]{1,2,0:T(1,128)S(1)} convert(s32[4,768,1]{1,2,0:T(1,128)} %param.13) | non-fusion elementwise | flops 3072 | bytes 24576 | tf_op jit(solution)/shard_map/convert_element_type | solution.py:376
  0.7 0.6 broadcast_in_dim.2.ids_ref
  1.4 61.9 %shard_map.73 = bf16[768,256]{1,0:T(8,128)(2,1)} custom-call(bf16[768,256]{1,0:T(8,128)(2,1)} %tok_ref.1, f32[1,1024]{1,0:T(1,128)} %bitcast.3, bf16[1024,256]{1,0:T(8,128)(2,1)} %wq_hbm.1, bf16[1024,256]{1,0:T(8,128)(2,1)} %wk_hbm.1, bf16[1024,256]{1,0:T(8,128)(2,1)} %wv_hbm.1, bf16[256,1024]{1,0:T(8,128)(2,1)} %wo_ref.1, ...), custom_call_target="tpu_custom_call" | custom-call | tf_op jit(solution)/shard_map/pallas_call | solution.py:381
  63.3 1.8 %copy.11 = bf16[768,256]{1,0:T(8,128)(2,1)} copy(bf16[768,256]{1,0:T(8,128)(2,1)} %shard_map.73) | data formatting | bytes 786432
  (2 shorter events, 0.0 us)
